TPU v7x, 32 devices: a whole 2x2x4 slice. The times are simulated.
32 devices in a mesh: section: 4 (over z), dp: 8 (over y, x, core).
Axes of the slice: x: 2, y: 2, z: 4, core: 2. Of those that a mesh axis runs over, the one named last changes fastest.
Arguments:
- images: bfloat16 [2, 1576, 1024], P(None, 'dp'), may hold values from -44 to 44
- cotangent: bfloat16 [2, 1576, 1024], P(None, 'dp'), may hold values from -0.75 to 0.75
- w_in: bfloat16 [4, 1024, 2048], P('section'), may hold values from -0.1875 to 0.1875
- w_out: bfloat16 [4, 2048, 1024], P('section'), may hold values from -0.125 to 0.125
- gain: float32 [4, 1024], P('section'), may hold values from 0.5 to 1.5
- shift: float32 [4, 1024], P('section'), may hold values from -3 to 3
Outputs:
- section_outputs: bfloat16 [4, 2, 1576, 1024], P('section', None, 'dp')
- input_grads: bfloat16 [4, 2, 1576, 1024], P('section', None, 'dp')
- grad_w_in: float32 [4, 1024, 2048], P('section', 'dp')
- grad_w_out: float32 [4, 2048, 1024], P('section', 'dp')
- grad_gain: float32 [4, 1024], P('section')
- grad_shift: float32 [4, 1024], P('section')
All inputs are finite; a program needn't handle non-finite values.
Results may differ from a plain program's by a relative error of at most 0.0095.
Values may be sent and summed in bfloat16 or wider, within the bound.
A program may use at most 192 MiB of HBM per device.

v0:
```python
import jax
import jax.numpy as jnp
from jax import lax
from jax.sharding import PartitionSpec as P

epsilon = 1e-05
gelu_scale = 0.7978845608028654
cubic_term = 0.044715


def from_behind(block, axis, distance):
    devices = range(lax.axis_size(axis))
    route = [(i - distance, i) for i in devices if i - distance in devices]
    return lax.ppermute(block, axis, route)


def gelu_parts(before):
    inner = gelu_scale * (before + cubic_term * before * before * before)
    bend = jnp.tanh(inner)
    value = 0.5 * before * (1.0 + bend)
    slope = 0.5 * (1.0 + bend) + 0.5 * before * (1.0 - bend * bend) * gelu_scale * (
        1.0 + 3.0 * cubic_term * before * before
    )
    return (value, slope)


def statistics(inputs, rows):
    total, squares = lax.psum((jnp.sum(inputs, axis=0), jnp.sum(inputs * inputs, axis=0)), "dp")
    mean = total / rows
    centered = inputs - mean
    spread = squares / rows - mean * mean
    return (centered, spread)


def pick(buffer, slot):
    return lax.dynamic_index_in_dim(buffer, slot, 0, keepdims=False)


def place(buffer, fresh, slot, valid):
    kept = pick(buffer, slot)
    return lax.dynamic_update_index_in_dim(buffer, jnp.where(valid, fresh, kept), slot, 0)


def local(images, cotangent, w_in, w_out, gain, shift):
    sections = lax.axis_size("section")
    section = lax.axis_index("section")
    micro = images.shape[0]
    rows_local = images.shape[1]
    width = images.shape[2]
    hidden_width = w_in.shape[2]
    rows = rows_local * lax.axis_size("dp")
    weight_in = w_in[0]
    weight_out = w_out[0]
    gain_row = gain[0]
    shift_row = shift[0]
    ticks = micro + sections - 1
    normed_buf = jnp.zeros((micro, rows_local, width), jnp.float32)
    inverse_buf = jnp.zeros((micro, width), jnp.float32)
    affine_buf = jnp.zeros((micro, rows_local, width), jnp.bfloat16)
    slope_buf = jnp.zeros((micro, rows_local, hidden_width), jnp.float32)
    active_buf = jnp.zeros((micro, rows_local, hidden_width), jnp.bfloat16)
    output_buf = jnp.zeros((micro, rows_local, width), jnp.bfloat16)
    arrived = jnp.zeros((rows_local, width), jnp.bfloat16)
    for tick in range(ticks):
        offset = tick - section
        valid = (offset >= 0) & (offset < micro)
        slot = jnp.clip(offset, 0, micro - 1)
        first = images[min(tick, micro - 1)]
        inputs = jnp.where(section == 0, first, arrived)
        inputs_f = inputs.astype(jnp.float32)
        centered, spread = statistics(inputs_f, rows)
        inverse = lax.rsqrt(spread + epsilon)
        normed = centered * inverse
        affine = (normed * gain_row + shift_row).astype(jnp.bfloat16)
        before = jnp.dot(affine, weight_in, preferred_element_type=jnp.float32)
        value, slope = gelu_parts(before)
        active = value.astype(jnp.bfloat16)
        output = (
            inputs_f + jnp.dot(active, weight_out, preferred_element_type=jnp.float32)
        ).astype(jnp.bfloat16)
        normed_buf = place(normed_buf, normed, slot, valid)
        inverse_buf = place(inverse_buf, inverse, slot, valid)
        affine_buf = place(affine_buf, affine, slot, valid)
        slope_buf = place(slope_buf, slope, slot, valid)
        active_buf = place(active_buf, active, slot, valid)
        output_buf = place(output_buf, output, slot, valid)
        if tick + 1 < ticks:
            arrived = from_behind(output, "section", 1)
    grad_in = jnp.zeros((width, hidden_width), jnp.float32)
    grad_out = jnp.zeros((hidden_width, width), jnp.float32)
    grad_gain = jnp.zeros((width,), jnp.float32)
    grad_shift = jnp.zeros((width,), jnp.float32)
    in_grad_buf = jnp.zeros((micro, rows_local, width), jnp.bfloat16)
    arrived = jnp.zeros((rows_local, width), jnp.bfloat16)
    for tick in range(ticks):
        offset = tick - (sections - 1 - section)
        valid = (offset >= 0) & (offset < micro)
        slot = jnp.clip(offset, 0, micro - 1)
        given = cotangent[min(tick, micro - 1)]
        upstream = jnp.where(section == sections - 1, given, arrived)
        normed = pick(normed_buf, slot)
        inverse = pick(inverse_buf, slot)
        affine = pick(affine_buf, slot)
        slope = pick(slope_buf, slot)
        active = pick(active_buf, slot)
        grad_out = grad_out + jnp.where(
            valid, jnp.dot(active.T, upstream, preferred_element_type=jnp.float32), 0.0
        )
        grad_active = jnp.dot(upstream, weight_out.T, preferred_element_type=jnp.float32)
        grad_before = (grad_active * slope).astype(jnp.bfloat16)
        grad_in = grad_in + jnp.where(
            valid, jnp.dot(affine.T, grad_before, preferred_element_type=jnp.float32), 0.0
        )
        grad_affine = jnp.dot(grad_before, weight_in.T, preferred_element_type=jnp.float32)
        sum_grad, sum_cross = lax.psum(
            (jnp.sum(grad_affine, axis=0), jnp.sum(grad_affine * normed, axis=0)), "dp"
        )
        grad_gain = grad_gain + jnp.where(valid, sum_cross, 0.0)
        grad_shift = grad_shift + jnp.where(valid, sum_grad, 0.0)
        grad_norm = inverse * gain_row * (grad_affine - sum_grad / rows - normed * sum_cross / rows)
        grad_inputs = (upstream.astype(jnp.float32) + grad_norm).astype(jnp.bfloat16)
        in_grad_buf = place(in_grad_buf, grad_inputs, slot, valid)
        if tick + 1 < ticks:
            arrived = from_behind(grad_inputs, "section", -1)
    reduced_in, reduced_out = (
        lax.psum_scatter(grad_in, "dp", scatter_dimension=0, tiled=True),
        lax.psum_scatter(grad_out, "dp", scatter_dimension=0, tiled=True),
    )
    return (
        output_buf[None],
        in_grad_buf[None],
        reduced_in[None],
        reduced_out[None],
        grad_gain[None],
        grad_shift[None],
    )


def solution(mesh):
    placed = (
        P(None, "dp", None),
        P(None, "dp", None),
        P("section", None, None),
        P("section", None, None),
        P("section", None),
        P("section", None),
    )
    return jax.shard_map(
        local,
        mesh=mesh,
        in_specs=placed,
        out_specs=(
            P("section", None, "dp", None),
            P("section", None, "dp", None),
            P("section", "dp", None),
            P("section", "dp", None),
            P("section", None),
            P("section", None),
        ),
        check_vma=False,
    )
```

profile of v0, /device:TPU:0, one launch (start us, length us, event | category | flops | bytes accessed | tf_op | source)
XLA Modules:
  0.0 493.0 jit_solution(13565825109413786812)
XLA Ops:
  7.2 3.7 fusion.285
  11.2 15.5 %all-reduce.9 = (f32[1024]{0:T(1024)S(1)}, f32[1024]{0:T(1024)S(1)}) all-reduce(f32[1024]{0:T(1024)S(1)} %fusion.146, f32[1024]{0:T(1024)S(1)} %get-tuple-element.65), channel_id=1, replica_groups=mesh['section'=4,'dp'=8] {'dp'}, use_global_device_ids=true, to_apply=%region_3.4 | all-reduce | flops 2048 | bytes 16384 | tf_op jit(solution)/shard_map/psum | solution.py:28
  27.7 4.2 fusion.85
  32.1 2.0 bitcast_dynamic-update-slice_fusion.16
  35.0 4.2 collective-permute-start
  40.2 1.9 select_dynamic-update-slice_fusion
  42.5 2.4 constant_dynamic-slice_fusion.7
  48.1 4.0 fusion.284
  53.3 12.1 %all-reduce.8 = (f32[1024]{0:T(1024)S(1)}, f32[1024]{0:T(1024)S(1)}) all-reduce(f32[1024]{0:T(1024)S(1)} %get-tuple-element.29, f32[1024]{0:T(1024)S(1)} %get-tuple-element.28), channel_id=1, replica_groups=mesh['section'=4,'dp'=8] {'dp'}, use_global_device_ids=true, to_apply=%region_7.8 | all-reduce | flops 2048 | bytes 16384 | tf_op jit(solution)/shard_map/psum | solution.py:28
  65.5 2.4 fusion.159
  68.9 4.9 fusion.91
  73.8 2.1 constant_dynamic-slice_fusion.6
  78.2 4.0 collective-permute-start.1
  84.6 6.0 %collective-permute-done.1 = bf16[197,1024]{1,0:T(8,128)(2,1)S(1)} collective-permute-done((bf16[197,1024]{1,0:T(8,128)(2,1)S(1)}, bf16[197,1024]{1,0:T(8,128)(2,1)S(1)}, u32[]{:S(2)}, u32[]{:S(2)}) %collective-permute-start.1) | collective-permute-done | bytes 403488 | tf_op jit(solution)/shard_map/ppermute | solution.py:14
  91.6 12.1 %all-reduce.7 = (f32[1024]{0:T(1024)S(1)}, f32[1024]{0:T(1024)S(1)}) all-reduce(f32[1024]{0:T(1024)S(1)} %get-tuple-element.27, f32[1024]{0:T(1024)S(1)} %get-tuple-element.26), channel_id=1, replica_groups=mesh['section'=4,'dp'=8] {'dp'}, use_global_device_ids=true, to_apply=%region_11.12 | all-reduce | flops 2048 | bytes 16384 | tf_op jit(solution)/shard_map/psum | solution.py:28
  103.7 2.4 fusion.167
  107.2 4.9 fusion.97
  112.1 2.1 constant_dynamic-slice_fusion.5
  116.5 4.4 collective-permute-start.2
  123.2 6.3 %collective-permute-done.2 = bf16[197,1024]{1,0:T(8,128)(2,1)S(1)} collective-permute-done((bf16[197,1024]{1,0:T(8,128)(2,1)S(1)}, bf16[197,1024]{1,0:T(8,128)(2,1)S(1)}, u32[]{:S(2)}, u32[]{:S(2)}) %collective-permute-start.2) | collective-permute-done | bytes 403488 | tf_op jit(solution)/shard_map/ppermute | solution.py:14
  130.4 12.1 %all-reduce.6 = (f32[1024]{0:T(1024)S(1)}, f32[1024]{0:T(1024)S(1)}) all-reduce(f32[1024]{0:T(1024)S(1)} %get-tuple-element.25, f32[1024]{0:T(1024)S(1)} %get-tuple-element.24), channel_id=1, replica_groups=mesh['section'=4,'dp'=8] {'dp'}, use_global_device_ids=true, to_apply=%region_15.16 | all-reduce | flops 2048 | bytes 16384 | tf_op jit(solution)/shard_map/psum | solution.py:28
  142.6 2.4 fusion.175
  146.0 4.9 fusion.103
  152.3 4.4 collective-permute-start.3
  156.7 1.8 constant_dynamic-slice_fusion.4
  160.9 4.5 collective-permute-done.3
  166.2 12.1 %all-reduce.5 = (f32[1024]{0:T(1024)S(1)}, f32[1024]{0:T(1024)S(1)}) all-reduce(f32[1024]{0:T(1024)S(1)} %get-tuple-element.23, f32[1024]{0:T(1024)S(1)} %get-tuple-element.22), channel_id=1, replica_groups=mesh['section'=4,'dp'=8] {'dp'}, use_global_device_ids=true, to_apply=%region_19.20 | all-reduce | flops 2048 | bytes 16384 | tf_op jit(solution)/shard_map/psum | solution.py:28
  178.4 2.4 fusion.183
  182.2 6.0 %fusion.109 = (f32[2,197,2048]{2,1,0:T(8,128)S(1)}, f32[197,2048]{1,0:T(8,128)}) fusion(f32[2,197,2048]{2,1,0:T(8,128)S(1)} %get-tuple-element.107, s32[]{:T(128)S(6)} %min.35, f32[1,197,2048]{2,1,0:T(8,128)} %constant_dynamic-slice_fusion.19, pred[]{:T(512)S(6)} %and.35, bf16[1,1024,2048]{2,1,0:T(8,128)(2,1)} %param.8, ...), kind=kOutput, calls=%fused_computation.101 | convolution fusion | flops 834750464 | bytes 9480197 | tf_op jit(solution)/shard_map/dot_general | solution.py:75
  190.9 2.4 fusion.279
  193.3 12.1 %all-reduce.4 = (f32[1024]{0:T(1024)S(1)}, f32[1024]{0:T(1024)S(1)}) all-reduce(f32[1024]{0:T(1024)S(1)} %get-tuple-element.21, f32[1024]{0:T(1024)S(1)} %get-tuple-element.20), channel_id=1, replica_groups=mesh['section'=4,'dp'=8] {'dp'}, use_global_device_ids=true, to_apply=%region_23.24 | all-reduce | flops 2048 | bytes 16384 | tf_op jit(solution)/shard_map/psum | solution.py:115
  205.6 2.1 bitcast_dynamic-update-slice_fusion.12
  210.2 5.8 %fusion.240 = f32[1024,2048]{1,0:T(8,128)} fusion(bf16[197,2048]{1,0:T(8,128)(2,1)S(1)} %copy-done.66, bf16[2,197,1024]{2,1,0:T(8,128)(2,1)} %bitcast_dynamic-update-slice_fusion.5, s32[]{:T(128)S(6)} %min.36), kind=kOutput, calls=%fused_computation.253 | convolution fusion | flops 826277888 | bytes 9605124 | tf_op jit(solution)/shard_map/dot_general | solution.py:112
  216.0 6.7 %collective-permute-done.4 = bf16[197,1024]{1,0:T(8,128)(2,1)S(1)} collective-permute-done((bf16[197,1024]{1,0:T(8,128)(2,1)S(1)}, bf16[197,1024]{1,0:T(8,128)(2,1)S(1)}, u32[]{:S(2)}, u32[]{:S(2)}) %collective-permute-start.4) | collective-permute-done | bytes 403488 | tf_op jit(solution)/shard_map/ppermute | solution.py:14
  226.4 2.4 fusion.278
  228.8 12.1 %all-reduce.3 = (f32[1024]{0:T(1024)S(1)}, f32[1024]{0:T(1024)S(1)}) all-reduce(f32[1024]{0:T(1024)S(1)} %get-tuple-element.19, f32[1024]{0:T(1024)S(1)} %get-tuple-element.18), channel_id=1, replica_groups=mesh['section'=4,'dp'=8] {'dp'}, use_global_device_ids=true, to_apply=%region_27.28 | all-reduce | flops 2048 | bytes 16384 | tf_op jit(solution)/shard_map/psum | solution.py:115
  241.0 2.8 bitcast_dynamic-update-slice_fusion.11
  243.7 1.8 constant_dynamic-slice_fusion.11
  247.1 5.7 %fusion.238 = f32[1024,2048]{1,0:T(8,128)} fusion(bf16[197,2048]{1,0:T(8,128)(2,1)S(1)} %copy-done.60, bf16[2,197,1024]{2,1,0:T(8,128)(2,1)} %bitcast_dynamic-update-slice_fusion.5, s32[]{:T(128)S(6)} %min.37), kind=kOutput, calls=%fused_computation.251 | convolution fusion | flops 826277888 | bytes 9605124 | tf_op jit(solution)/shard_map/dot_general | solution.py:112
  252.9 5.8 %collective-permute-done.5 = bf16[197,1024]{1,0:T(8,128)(2,1)S(1)} collective-permute-done((bf16[197,1024]{1,0:T(8,128)(2,1)S(1)}, bf16[197,1024]{1,0:T(8,128)(2,1)S(1)}, u32[]{:S(2)}, u32[]{:S(2)}) %collective-permute-start.5) | collective-permute-done | bytes 403488 | tf_op jit(solution)/shard_map/ppermute | solution.py:14
  261.6 2.4 fusion.277
  264.0 12.1 %all-reduce.2 = (f32[1024]{0:T(1024)S(1)}, f32[1024]{0:T(1024)S(1)}) all-reduce(f32[1024]{0:T(1024)S(1)} %get-tuple-element.17, f32[1024]{0:T(1024)S(1)} %get-tuple-element.16), channel_id=1, replica_groups=mesh['section'=4,'dp'=8] {'dp'}, use_global_device_ids=true, to_apply=%region_31.32 | all-reduce | flops 2048 | bytes 16384 | tf_op jit(solution)/shard_map/psum | solution.py:115
  276.1 2.8 bitcast_dynamic-update-slice_fusion.10
  278.8 1.8 constant_dynamic-slice_fusion.9
  282.1 5.8 %fusion.236 = f32[1024,2048]{1,0:T(8,128)} fusion(bf16[197,2048]{1,0:T(8,128)(2,1)S(1)} %copy-done.62, bf16[2,197,1024]{2,1,0:T(8,128)(2,1)} %bitcast_dynamic-update-slice_fusion.5, s32[]{:T(128)S(6)} %min.38), kind=kOutput, calls=%fused_computation.249 | convolution fusion | flops 826277888 | bytes 9605124 | tf_op jit(solution)/shard_map/dot_general | solution.py:112
  287.9 5.9 %collective-permute-done.6 = bf16[197,1024]{1,0:T(8,128)(2,1)S(1)} collective-permute-done((bf16[197,1024]{1,0:T(8,128)(2,1)S(1)}, bf16[197,1024]{1,0:T(8,128)(2,1)S(1)}, u32[]{:S(2)}, u32[]{:S(2)}) %collective-permute-start.6) | collective-permute-done | bytes 403488 | tf_op jit(solution)/shard_map/ppermute | solution.py:14
  296.7 2.4 fusion.276
  299.1 12.1 %all-reduce.1 = (f32[1024]{0:T(1024)S(1)}, f32[1024]{0:T(1024)S(1)}) all-reduce(f32[1024]{0:T(1024)S(1)} %get-tuple-element.15, f32[1024]{0:T(1024)S(1)} %get-tuple-element.14), channel_id=1, replica_groups=mesh['section'=4,'dp'=8] {'dp'}, use_global_device_ids=true, to_apply=%region_35.36 | all-reduce | flops 2048 | bytes 16384 | tf_op jit(solution)/shard_map/psum | solution.py:115
  311.2 2.8 bitcast_dynamic-update-slice_fusion.9
  315.4 2.5 fusion.234
  317.9 9.2 %collective-permute-done.7 = bf16[197,1024]{1,0:T(8,128)(2,1)S(1)} collective-permute-done((bf16[197,1024]{1,0:T(8,128)(2,1)S(1)}, bf16[197,1024]{1,0:T(8,128)(2,1)S(1)}, u32[]{:S(2)}, u32[]{:S(2)}) %collective-permute-start.7) | collective-permute-done | bytes 403488 | tf_op jit(solution)/shard_map/ppermute | solution.py:14
  330.4 6.0 %select_add_fusion.1 = f32[1024,2048]{1,0:T(8,128)} fusion(f32[1024,2048]{1,0:T(8,128)S(1)} %fusion.234, f32[1024,2048]{1,0:T(8,128)} %fusion.236, f32[1024,2048]{1,0:T(8,128)} %fusion.238, f32[1024,2048]{1,0:T(8,128)} %fusion.240, bf16[197,2048]{1,0:T(8,128)(2,1)S(1)} %fusion.55, pred[]{:T(512)S(6)} %and.40, pred[]{:T(512)S(6)} %and.39, pred[]{:T(512)S(6)} %and.38, ...), kind=kOutput, calls=%fused_computation.1 | convolution fusion | flops 845152256 | bytes 43159560 | tf_op jit(solution)/shard_map/dot_general | solution.py:112
  348.3 5.6 %fusion.190 = f32[2048,1024]{1,0:T(8,128)} fusion(bf16[197,1024]{1,0:T(8,128)(2,1)S(1)} %copy-done.35, bf16[2,197,2048]{2,1,0:T(8,128)(2,1)S(1)} %bitcast_dynamic-update-slice_fusion, s32[]{:T(128)S(6)} %min.37), kind=kOutput, calls=%fused_computation.180 | convolution fusion | flops 826277888 | bytes 9617412 | tf_op jit(solution)/shard_map/dot_general | solution.py:107
  353.9 4.6 fusion.188
  358.5 4.6 fusion.186
  363.1 7.7 %select_add_fusion = f32[2048,1024]{1,0:T(8,128)} fusion(f32[2048,1024]{1,0:T(8,128)} %fusion.186, f32[2048,1024]{1,0:T(8,128)} %fusion.188, f32[2048,1024]{1,0:T(8,128)} %fusion.190, f32[2048,1024]{1,0:T(8,128)S(1)} %fusion.192, bf16[197,1024]{1,0:T(8,128)(2,1)S(1)} %copy-done.32, pred[]{:T(512)S(6)} %and.40, pred[]{:T(512)S(6)} %and.39, pred[]{:T(512)S(6)} %and.38, ...), kind=kOutput, calls=%fused_computation | convolution fusion | flops 845152256 | bytes 43171848 | tf_op jit(solution)/shard_map/dot_general | solution.py:107
  372.1 4.3 fusion.142
  376.4 1.7 copy.35
  379.0 2.4 fusion.275
  381.4 12.4 %all-reduce = (f32[1024]{0:T(1024)S(1)}, f32[1024]{0:T(1024)S(1)}) all-reduce(f32[1024]{0:T(1024)S(1)} %get-tuple-element.13, f32[1024]{0:T(1024)S(1)} %get-tuple-element.12), channel_id=1, replica_groups=mesh['section'=4,'dp'=8] {'dp'}, use_global_device_ids=true, to_apply=%region_39.40 | all-reduce | flops 2048 | bytes 16384 | tf_op jit(solution)/shard_map/psum | solution.py:115
  394.4 2.4 fusion.231
  396.8 2.9 copy.36
  399.7 10.2 %reduce-scatter.3.cloned.1.call-done = f32[128,2048]{1,0:T(8,128)} async-done(((f32[1024,2048]{1,0:T(8,128)}), f32[128,2048]{1,0:T(8,128)}) %reduce-scatter.3.cloned.1.call-update) | async-done | bytes 1048592 | tf_op jit(solution)/shard_map/reduce_scatter | solution.py:126
  409.9 75.8 %reduce-scatter.5.cloned.1.call-done = f32[256,1024]{1,0:T(8,128)} async-done(((f32[2048,1024]{1,0:T(8,128)}), f32[256,1024]{1,0:T(8,128)}) %reduce-scatter.5.cloned.1.call-update) | async-done | bytes 1048592 | tf_op jit(solution)/shard_map/reduce_scatter | solution.py:127
  (267 shorter events, 65.1 us)
Async XLA Ops:
  7.2 402.8 %reduce-scatter.3.cloned.1.call-start = ((), (), s32[]{:S(2)}) async-start(), calls=%async_computation.2 | async-start | bytes 9437184 | tf_op jit(solution)/shard_map/reduce_scatter | solution.py:126
  11.1 15.6 %copy-start.43 = (bf16[1,197,1024]{2,1,0:T(8,128)(2,1)}, bf16[1,197,1024]{2,1,0:T(8,128)(2,1)S(1)}, u32[]{:S(2)}) copy-start(bf16[1,197,1024]{2,1,0:T(8,128)(2,1)S(1)} %get-tuple-element.66) | copy-start | bytes 1210372
  27.7 4.4 copy-start
  35.0 17.1 %collective-permute-start = (bf16[197,1024]{1,0:T(8,128)(2,1)}, bf16[197,1024]{1,0:T(8,128)(2,1)}, u32[]{:S(2)}, u32[]{:S(2)}) collective-permute-start(bf16[197,1024]{1,0:T(8,128)(2,1)} %get-tuple-element.94), channel_id=1, source_target_pairs={{0,8},{8,16},{16,24},{1,9},{9,17},{17,25},{2,10},{10,18},{18,26},{... | collective-permute-start | bytes 1210376 | tf_op jit(solution)/shard_map/ppermute | solution.py:14
  39.2 3.1 copy-start.45
  42.4 3.5 copy-start.21
  42.5 4.2 copy-start.9
  48.1 4.0 copy-start.68
  68.9 7.1 %copy-start.1 = (bf16[1,2048,1024]{2,1,0:T(8,128)(2,1)S(1)}, bf16[1,2048,1024]{2,1,0:T(8,128)(2,1)}, u32[]{:S(2)}) copy-start(bf16[1,2048,1024]{2,1,0:T(8,128)(2,1)} %param.9) | copy-start | bytes 12582916
  68.9 7.1 %copy-start.22 = (bf16[2,197,1024]{2,1,0:T(8,128)(2,1)S(1)}, bf16[2,197,1024]{2,1,0:T(8,128)(2,1)}, u32[]{:S(2)}) copy-start(bf16[2,197,1024]{2,1,0:T(8,128)(2,1)} %copy-done.20) | copy-start | bytes 2420740
  68.9 7.1 %copy-start.56 = (bf16[197,1024]{1,0:T(8,128)(2,1)S(1)}, bf16[197,1024]{1,0:T(8,128)(2,1)}, u32[]{:S(2)}) copy-start(bf16[197,1024]{1,0:T(8,128)(2,1)} %get-tuple-element.63) | copy-start | bytes 1210372
  68.9 7.0 %copy-start.82 = (bf16[1,197,1024]{2,1,0:T(8,128)(2,1)S(1)}, bf16[1,197,1024]{2,1,0:T(8,128)(2,1)}, u32[]{:S(2)}) copy-start(bf16[1,197,1024]{2,1,0:T(8,128)(2,1)} %constant_dynamic-slice_fusion.30) | copy-start | bytes 1210372
  73.8 3.5 copy-start.71
  76.0 6.3 %copy-start.10 = (f32[2,197,1024]{2,1,0:T(8,128)S(1)}, f32[2,197,1024]{2,1,0:T(8,128)}, u32[]{:S(2)}) copy-start(f32[2,197,1024]{2,1,0:T(8,128)} %fusion.159) | copy-start | bytes 4841476
  77.3 6.0 %copy-start.23 = (bf16[2,197,1024]{2,1,0:T(8,128)(2,1)}, bf16[2,197,1024]{2,1,0:T(8,128)(2,1)S(1)}, u32[]{:S(2)}) copy-start(bf16[2,197,1024]{2,1,0:T(8,128)(2,1)S(1)} %get-tuple-element.95) | copy-start | bytes 2420740
  78.2 12.4 %collective-permute-start.1 = (bf16[197,1024]{1,0:T(8,128)(2,1)S(1)}, bf16[197,1024]{1,0:T(8,128)(2,1)S(1)}, u32[]{:S(2)}, u32[]{:S(2)}) collective-permute-start(bf16[197,1024]{1,0:T(8,128)(2,1)S(1)} %get-tuple-element.96), channel_id=1, source_target_pairs={{0,8},{8,16},{16,24},{1,9},{9,17},{17,25},{2,10},{10,18},{18,26},{... | collective-permute-start | bytes 1210376 | tf_op jit(solution)/shard_map/ppermute | solution.py:14
  83.2 7.4 %copy-start.40 = (bf16[197,1024]{1,0:T(8,128)(2,1)S(1)}, bf16[197,1024]{1,0:T(8,128)(2,1)}, u32[]{:S(2)}) copy-start(bf16[197,1024]{1,0:T(8,128)(2,1)} %get-tuple-element.64) | copy-start | bytes 1210372
  107.1 7.1 %copy-start.2 = (bf16[1,2048,1024]{2,1,0:T(8,128)(2,1)S(1)}, bf16[1,2048,1024]{2,1,0:T(8,128)(2,1)}, u32[]{:S(2)}) copy-start(bf16[1,2048,1024]{2,1,0:T(8,128)(2,1)} %param.9) | copy-start | bytes 12582916
  107.1 7.1 %copy-start.24 = (bf16[2,197,1024]{2,1,0:T(8,128)(2,1)S(1)}, bf16[2,197,1024]{2,1,0:T(8,128)(2,1)}, u32[]{:S(2)}) copy-start(bf16[2,197,1024]{2,1,0:T(8,128)(2,1)} %copy-done.23) | copy-start | bytes 2420740
  107.1 7.1 %copy-start.52 = (bf16[197,1024]{1,0:T(8,128)(2,1)S(1)}, bf16[197,1024]{1,0:T(8,128)(2,1)}, u32[]{:S(2)}) copy-start(bf16[197,1024]{1,0:T(8,128)(2,1)} %get-tuple-element.62) | copy-start | bytes 1210372
  107.2 7.0 %copy-start.83 = (bf16[1,197,1024]{2,1,0:T(8,128)(2,1)S(1)}, bf16[1,197,1024]{2,1,0:T(8,128)(2,1)}, u32[]{:S(2)}) copy-start(bf16[1,197,1024]{2,1,0:T(8,128)(2,1)} %constant_dynamic-slice_fusion.29) | copy-start | bytes 1210372
  112.1 3.5 copy-start.73
  114.2 6.7 %copy-start.11 = (f32[2,197,1024]{2,1,0:T(8,128)S(1)}, f32[2,197,1024]{2,1,0:T(8,128)}, u32[]{:S(2)}) copy-start(f32[2,197,1024]{2,1,0:T(8,128)} %fusion.167) | copy-start | bytes 4841476
  115.5 6.3 %copy-start.25 = (bf16[2,197,1024]{2,1,0:T(8,128)(2,1)}, bf16[2,197,1024]{2,1,0:T(8,128)(2,1)S(1)}, u32[]{:S(2)}) copy-start(bf16[2,197,1024]{2,1,0:T(8,128)(2,1)S(1)} %get-tuple-element.97) | copy-start | bytes 2420740
  116.5 13.0 %collective-permute-start.2 = (bf16[197,1024]{1,0:T(8,128)(2,1)S(1)}, bf16[197,1024]{1,0:T(8,128)(2,1)S(1)}, u32[]{:S(2)}, u32[]{:S(2)}) collective-permute-start(bf16[197,1024]{1,0:T(8,128)(2,1)S(1)} %get-tuple-element.98), channel_id=1, source_target_pairs={{0,8},{8,16},{16,24},{1,9},{9,17},{17,25},{2,10},{10,18},{18,26},{... | collective-permute-start | bytes 1210376 | tf_op jit(solution)/shard_map/ppermute | solution.py:14
  121.8 7.6 %copy-start.41 = (bf16[197,1024]{1,0:T(8,128)(2,1)S(1)}, bf16[197,1024]{1,0:T(8,128)(2,1)}, u32[]{:S(2)}) copy-start(bf16[197,1024]{1,0:T(8,128)(2,1)} %get-tuple-element.64) | copy-start | bytes 1210372
  145.9 5.0 %copy-start.3 = (bf16[1,2048,1024]{2,1,0:T(8,128)(2,1)S(1)}, bf16[1,2048,1024]{2,1,0:T(8,128)(2,1)}, u32[]{:S(2)}) copy-start(bf16[1,2048,1024]{2,1,0:T(8,128)(2,1)} %param.9) | copy-start | bytes 12582916
  146.0 5.0 %copy-start.26 = (bf16[2,197,1024]{2,1,0:T(8,128)(2,1)S(1)}, bf16[2,197,1024]{2,1,0:T(8,128)(2,1)}, u32[]{:S(2)}) copy-start(bf16[2,197,1024]{2,1,0:T(8,128)(2,1)} %copy-done.25) | copy-start | bytes 2420740
  146.0 5.0 %copy-start.54 = (bf16[197,1024]{1,0:T(8,128)(2,1)S(1)}, bf16[197,1024]{1,0:T(8,128)(2,1)}, u32[]{:S(2)}) copy-start(bf16[197,1024]{1,0:T(8,128)(2,1)} %get-tuple-element.61) | copy-start | bytes 1210372
  146.0 5.0 %copy-start.84 = (bf16[1,197,1024]{2,1,0:T(8,128)(2,1)S(1)}, bf16[1,197,1024]{2,1,0:T(8,128)(2,1)}, u32[]{:S(2)}) copy-start(bf16[1,197,1024]{2,1,0:T(8,128)(2,1)} %constant_dynamic-slice_fusion.28) | copy-start | bytes 1210372
  151.0 7.6 %copy-start.12 = (f32[2,197,1024]{2,1,0:T(8,128)S(1)}, f32[2,197,1024]{2,1,0:T(8,128)}, u32[]{:S(2)}) copy-start(f32[2,197,1024]{2,1,0:T(8,128)} %fusion.175) | copy-start | bytes 4841476
  152.3 7.2 %copy-start.27 = (bf16[2,197,1024]{2,1,0:T(8,128)(2,1)}, bf16[2,197,1024]{2,1,0:T(8,128)(2,1)S(1)}, u32[]{:S(2)}) copy-start(bf16[2,197,1024]{2,1,0:T(8,128)(2,1)S(1)} %get-tuple-element.99) | copy-start | bytes 2420740
  152.3 13.0 %collective-permute-start.3 = (bf16[197,1024]{1,0:T(8,128)(2,1)S(1)}, bf16[197,1024]{1,0:T(8,128)(2,1)S(1)}, u32[]{:S(2)}, u32[]{:S(2)}) collective-permute-start(bf16[197,1024]{1,0:T(8,128)(2,1)S(1)} %get-tuple-element.100), channel_id=1, source_target_pairs={{0,8},{8,16},{16,24},{1,9},{9,17},{17,25},{2,10},{10,18},{18,26},{... | collective-permute-start | bytes 1210376 | tf_op jit(solution)/shard_map/ppermute | solution.py:14
  159.5 5.8 %copy-start.42 = (bf16[197,1024]{1,0:T(8,128)(2,1)S(1)}, bf16[197,1024]{1,0:T(8,128)(2,1)}, u32[]{:S(2)}) copy-start(bf16[197,1024]{1,0:T(8,128)(2,1)} %get-tuple-element.64) | copy-start | bytes 1210372
  182.2 6.0 %copy-start.4 = (bf16[1,2048,1024]{2,1,0:T(8,128)(2,1)S(1)}, bf16[1,2048,1024]{2,1,0:T(8,128)(2,1)}, u32[]{:S(2)}) copy-start(bf16[1,2048,1024]{2,1,0:T(8,128)(2,1)} %param.9) | copy-start | bytes 12582916
  182.2 6.0 %copy-start.29 = (bf16[1,197,1024]{2,0,1:T(2,128)(2,1)S(1)}, bf16[1,197,1024]{2,0,1:T(2,128)(2,1)}, u32[]{:S(2)}) copy-start(bf16[1,197,1024]{2,0,1:T(2,128)(2,1)} %get-tuple-element.68) | copy-start | bytes 1210372
  188.2 2.7 copy-start.87
  205.6 4.6 copy-start.66
  208.8 13.9 %copy-start.67 = (bf16[1,197,1024]{2,0,1:T(2,128)(2,1)S(1)}, bf16[1,197,1024]{2,0,1:T(2,128)(2,1)}, u32[]{:S(2)}) copy-start(bf16[1,197,1024]{2,0,1:T(2,128)(2,1)} %get-tuple-element.67) | copy-start | bytes 1210372
  208.8 13.9 %collective-permute-start.4 = (bf16[197,1024]{1,0:T(8,128)(2,1)S(1)}, bf16[197,1024]{1,0:T(8,128)(2,1)S(1)}, u32[]{:S(2)}, u32[]{:S(2)}) collective-permute-start(bf16[197,1024]{1,0:T(8,128)(2,1)S(1)} %get-tuple-element.59), channel_id=1, source_target_pairs={{8,0},{16,8},{24,16},{9,1},{17,9},{25,17},{10,2},{18,10},{26,18},{... | collective-permute-start | bytes 1210376 | tf_op jit(solution)/shard_map/ppermute | solution.py:14
  210.2 13.4 %copy-start.5 = (bf16[1,2048,1024]{2,1,0:T(8,128)(2,1)S(1)}, bf16[1,2048,1024]{2,1,0:T(8,128)(2,1)}, u32[]{:S(2)}) copy-start(bf16[1,2048,1024]{2,1,0:T(8,128)(2,1)} %param.9) | copy-start | bytes 12582916
  223.6 2.8 copy-start.88
  240.9 6.2 %copy-start.60 = (bf16[197,2048]{1,0:T(8,128)(2,1)S(1)}, bf16[197,2048]{1,0:T(8,128)(2,1)}, u32[]{:S(2)}) copy-start(bf16[197,2048]{1,0:T(8,128)(2,1)} %copy-done.59) | copy-start | bytes 2420740
  245.5 13.1 %copy-start.46 = (bf16[197,1024]{1,0:T(8,128)(2,1)S(1)}, bf16[197,1024]{1,0:T(8,128)(2,1)}, u32[]{:S(2)}) copy-start(bf16[197,1024]{1,0:T(8,128)(2,1)} %get-tuple-element.57) | copy-start | bytes 1210372
  245.5 13.1 %collective-permute-start.5 = (bf16[197,1024]{1,0:T(8,128)(2,1)S(1)}, bf16[197,1024]{1,0:T(8,128)(2,1)S(1)}, u32[]{:S(2)}, u32[]{:S(2)}) collective-permute-start(bf16[197,1024]{1,0:T(8,128)(2,1)S(1)} %get-tuple-element.55), channel_id=1, source_target_pairs={{8,0},{16,8},{24,16},{9,1},{17,9},{25,17},{10,2},{18,10},{26,18},{... | collective-permute-start | bytes 1210376 | tf_op jit(solution)/shard_map/ppermute | solution.py:14
  247.1 11.6 %copy-start.6 = (bf16[1,2048,1024]{2,1,0:T(8,128)(2,1)S(1)}, bf16[1,2048,1024]{2,1,0:T(8,128)(2,1)}, u32[]{:S(2)}) copy-start(bf16[1,2048,1024]{2,1,0:T(8,128)(2,1)} %param.9) | copy-start | bytes 12582916
  258.7 2.8 copy-start.89
  276.1 6.0 %copy-start.62 = (bf16[197,2048]{1,0:T(8,128)(2,1)S(1)}, bf16[197,2048]{1,0:T(8,128)(2,1)}, u32[]{:S(2)}) copy-start(bf16[197,2048]{1,0:T(8,128)(2,1)} %copy-done.61) | copy-start | bytes 2420740
  280.7 13.1 %copy-start.47 = (bf16[197,1024]{1,0:T(8,128)(2,1)S(1)}, bf16[197,1024]{1,0:T(8,128)(2,1)}, u32[]{:S(2)}) copy-start(bf16[197,1024]{1,0:T(8,128)(2,1)} %get-tuple-element.57) | copy-start | bytes 1210372
  280.7 13.1 %collective-permute-start.6 = (bf16[197,1024]{1,0:T(8,128)(2,1)S(1)}, bf16[197,1024]{1,0:T(8,128)(2,1)S(1)}, u32[]{:S(2)}, u32[]{:S(2)}) collective-permute-start(bf16[197,1024]{1,0:T(8,128)(2,1)S(1)} %get-tuple-element.53), channel_id=1, source_target_pairs={{8,0},{16,8},{24,16},{9,1},{17,9},{25,17},{10,2},{18,10},{26,18},{... | collective-permute-start | bytes 1210376 | tf_op jit(solution)/shard_map/ppermute | solution.py:14
  282.1 11.8 %copy-start.7 = (bf16[1,2048,1024]{2,1,0:T(8,128)(2,1)S(1)}, bf16[1,2048,1024]{2,1,0:T(8,128)(2,1)}, u32[]{:S(2)}) copy-start(bf16[1,2048,1024]{2,1,0:T(8,128)(2,1)} %param.9) | copy-start | bytes 12582916
  293.9 2.8 copy-start.90
  311.2 4.2 copy-start.64
  314.0 13.1 %copy-start.48 = (bf16[197,1024]{1,0:T(8,128)(2,1)S(1)}, bf16[197,1024]{1,0:T(8,128)(2,1)}, u32[]{:S(2)}) copy-start(bf16[197,1024]{1,0:T(8,128)(2,1)} %get-tuple-element.57) | copy-start | bytes 1210372
  314.0 13.1 %collective-permute-start.7 = (bf16[197,1024]{1,0:T(8,128)(2,1)S(1)}, bf16[197,1024]{1,0:T(8,128)(2,1)S(1)}, u32[]{:S(2)}, u32[]{:S(2)}) collective-permute-start(bf16[197,1024]{1,0:T(8,128)(2,1)S(1)} %get-tuple-element.51), channel_id=1, source_target_pairs={{8,0},{16,8},{24,16},{9,1},{17,9},{25,17},{10,2},{18,10},{26,18},{... | collective-permute-start | bytes 1210376 | tf_op jit(solution)/shard_map/ppermute | solution.py:14
  315.4 12.5 %copy-start.8 = (bf16[1,2048,1024]{2,1,0:T(8,128)(2,1)S(1)}, bf16[1,2048,1024]{2,1,0:T(8,128)(2,1)}, u32[]{:S(2)}) copy-start(bf16[1,2048,1024]{2,1,0:T(8,128)(2,1)} %param.9) | copy-start | bytes 12582916
  336.4 149.3 %reduce-scatter.5.cloned.1.call-start = ((), (), s32[]{:S(2)}) async-start(), calls=%async_computation.3 | async-start | bytes 9437184 | tf_op jit(solution)/shard_map/reduce_scatter | solution.py:127
  348.3 5.7 %copy-start.37 = (bf16[197,1024]{1,0:T(8,128)(2,1)S(1)}, bf16[197,1024]{1,0:T(8,128)(2,1)}, u32[]{:S(2)}) copy-start(bf16[197,1024]{1,0:T(8,128)(2,1)} %copy-done.36) | copy-start | bytes 1210372
  353.9 4.6 copy-start.39
  358.5 4.6 copy-start.32
  372.1 6.1 %copy-start.19 = (bf16[2,197,1024]{2,1,0:T(8,128)(2,1)S(1)}, bf16[2,197,1024]{2,1,0:T(8,128)(2,1)}, u32[]{:S(2)}) copy-start(bf16[2,197,1024]{2,1,0:T(8,128)(2,1)} %get-tuple-element.50) | copy-start | bytes 2420740
  372.1 6.9 %copy-start.91 = (bf16[1,1024,2048]{2,1,0:T(8,128)(2,1)S(1)}, bf16[1,1024,2048]{2,1,0:T(8,128)(2,1)}, u32[]{:S(2)}) copy-start(bf16[1,1024,2048]{2,1,0:T(8,128)(2,1)} %param.8) | copy-start | bytes 12582916
  376.4 2.6 copy-start.17
  379.0 15.4 %copy-start.33 = (bf16[197,1024]{1,0:T(8,128)(2,1)S(1)}, bf16[197,1024]{1,0:T(8,128)(2,1)}, u32[]{:S(2)}) copy-start(bf16[197,1024]{1,0:T(8,128)(2,1)} %copy-done.31) | copy-start | bytes 1210372
  (38 other events, 64.9 us)
Sparse Core Ops, SparseCore 0:
  336.5 73.4 reduce-scatter.2
  414.4 71.2 reduce-scatter.4
where the time goes:
time: 503 us; the launch traced here: 493 us
  waiting for transfers between devices  130 us (26%)
  blocking collectives  125 us (25%)
  matrix products  104 us (21%)
  local copies, waits for them, and re-layouts  57.2 us (11%)
  other arithmetic  37.6 us (7%)
  starting transfers between devices  23.2 us (5%)
  between operations  15.8 us (3%)
    reduce_scatter x1, waiting for transfers between devices, local(): lax.psum_scatter(grad_out, 'dp', scatter_dimension=0, tiled=True)  75.8 us
    psum x5, blocking collectives, statistics(): lax.psum((jnp.sum(inputs, axis=0), jnp.sum(inputs * inputs, axis=0)), 'dp')  63.8 us
    psum x5, blocking collectives, local(): lax.psum((jnp.sum(grad_affine, axis=0), jnp.sum(grad_affine * normed, axi...  60.8 us
    ppermute x8, waiting for transfers between devices, from_behind(): return lax.ppermute(block, axis, route)  44.3 us
    dynamic_update_slice x20, other arithmetic, place(): lax.dynamic_update_index_in_dim(buffer, jnp.where(valid, fresh, kept), sl...  31.5 us
    dot_general x5, matrix products, local(): jnp.dot(affine.T, grad_before, preferred_element_type=jnp.float32)  25.7 us
    dynamic_slice x26, local copies, waits for them, and re-layouts, pick(): return lax.dynamic_index_in_dim(buffer, slot, 0, keepdims=False)  25.1 us
    dot_general x5, matrix products, local(): before = jnp.dot(affine, weight_in, preferred_element_type=jnp.float32)  24.9 us
  transfers between devices with their start and end apart: 10, of which 9 were waited for; matrix products, arithmetic and copies ran while one was open for 17% of the time, Pallas kernels for 0%

commit v1 on v0

v1 whole, which is shorter than its diff:
```python
import functools

import jax
import jax.numpy as jnp
from jax import lax
from jax.experimental import pallas as pl
from jax.experimental.pallas import tpu as pltpu
from jax.sharding import PartitionSpec as P

epsilon = 1e-05
gelu_scale = 0.7978845608028654
cubic_term = 0.044715
f32 = jnp.float32
bf16 = jnp.bfloat16
MESH = pl.DeviceIdType.MESH


def near_square(count):
    side = int(count**0.5)
    while count % side:
        side -= 1
    return side


def loop(count, body):
    def step(i, carry):
        body(i)
        return carry

    lax.fori_loop(0, count, step, 0)


def cut(j, size):
    return pl.ds(pl.multiple_of(j * size, size), size)


def across(lhs, rhs):
    return lax.dot_general(lhs, rhs, (((1,), (1,)), ((), ())), preferred_element_type=f32)


def kernel(
    sizes,
    images, cotangent, w_in, w_out, gain, shift,
    out, gin, red_in, red_out, ggain, gshift,
    xbuf, ubuf, stat, stat_out, ex, aff, active, slope, gb, ga_buf, act_t, aff_t,
    send_i, keep_i, r0_i, r1_i, r2_i,
    send_o, keep_o, r0_o, r1_o, r2_o,
    x_send, x_recv, u_send, u_recv, st_send, st_recv, ex_send, ex_recv,
    s0, q0, s1, q1, s2, q2,
):
    sections, n, micro, real, rp, width, hidden, nx, ny = sizes
    rows = real * n
    wt = min(256, width)
    ht = min(512, hidden)
    nw = width // wt
    nh = hidden // ht
    section = lax.axis_index("section")
    me = lax.axis_index("dp")
    first = section == 0
    last = section == sections - 1
    not_first = section > 0
    not_last = section < sections - 1

    barrier = pltpu.get_barrier_semaphore()

    def greet(k):
        pl.semaphore_signal(
            barrier, inc=1, device_id={"dp": lax.rem(me + k + 1, n)}, device_id_type=MESH
        )

    loop(n - 1, greet)

    @pl.when(not_first)
    def _():
        pl.semaphore_signal(barrier, inc=1, device_id={"section": section - 1}, device_id_type=MESH)

    @pl.when(not_last)
    def _():
        pl.semaphore_signal(barrier, inc=1, device_id={"section": section + 1}, device_id_type=MESH)

    peers = n - 1 + not_first.astype(jnp.int32) + not_last.astype(jnp.int32)
    pl.semaphore_wait(barrier, peers)

    valid = lax.broadcasted_iota(jnp.int32, (rp, wt), 0) < real

    def local_stats(kind, m, j, tile):
        mean = jnp.sum(tile, axis=0, keepdims=True) / real
        gap = jnp.where(valid, tile - mean, 0.0)
        ex[kind, m, me, 0:1, cut(j, wt)] = mean
        ex[kind, m, me, 1:2, cut(j, wt)] = jnp.sum(gap * gap, axis=0, keepdims=True)

    def ex_copy(kind, m, k, slot):
        return pltpu.make_async_remote_copy(
            src_ref=ex.at[kind, m, slot],
            dst_ref=ex.at[kind, m, slot],
            send_sem=ex_send.at[kind, m, k],
            recv_sem=ex_recv.at[kind, m, k],
            device_id={"dp": lax.rem(me + k + 1, n)},
            device_id_type=MESH,
        )

    def ex_start(kind, m):
        loop(n - 1, lambda k: ex_copy(kind, m, k, me).start())

    def ex_wait(kind, m):
        loop(n - 1, lambda k: ex_copy(kind, m, k, lax.rem(me - k - 1 + n, n)).wait_recv())
        loop(n - 1, lambda k: ex_copy(kind, m, k, me).wait_send())
        return ex[kind, m]

    def combine(kind, m, target):
        parts = ex_wait(kind, m)
        means = parts[:, 0, :]
        mean = jnp.sum(means, axis=0, keepdims=True) / n
        gap = means - mean
        spread = (
            jnp.sum(parts[:, 1, :], axis=0, keepdims=True)
            + real * jnp.sum(gap * gap, axis=0, keepdims=True)
        ) / rows
        target[m, 0:1, :] = mean
        target[m, 1:2, :] = lax.rsqrt(spread + epsilon)

    def x_copy(m, j):
        return pltpu.make_async_remote_copy(
            src_ref=out.at[0, m, :, cut(j, wt)],
            dst_ref=xbuf.at[m, :, cut(j, wt)],
            send_sem=x_send.at[m, j],
            recv_sem=x_recv.at[m, j],
            device_id={"section": section + 1},
            device_id_type=MESH,
        )

    def u_copy(m, j):
        return pltpu.make_async_remote_copy(
            src_ref=gin.at[0, m, :, cut(j, wt)],
            dst_ref=ubuf.at[m, :, cut(j, wt)],
            send_sem=u_send.at[m, j],
            recv_sem=u_recv.at[m, j],
            device_id={"section": section - 1},
            device_id_type=MESH,
        )

    def st_copy(m):
        return pltpu.make_async_remote_copy(
            src_ref=stat_out.at[m],
            dst_ref=stat.at[m],
            send_sem=st_send.at[m],
            recv_sem=st_recv.at[m],
            device_id={"section": section + 1},
            device_id_type=MESH,
        )

    ggain[...] = jnp.zeros_like(ggain)
    gshift[...] = jnp.zeros_like(gshift)

    @pl.when(first)
    def _():
        for m in range(micro):
            xbuf[m, rp - 16 : rp, :] = jnp.zeros((16, width), bf16)
            xbuf[m, 0:real, :] = images[m]

            def tile(j):
                local_stats(0, m, j, xbuf[m, :, cut(j, wt)].astype(f32))

            loop(nw, tile)
            ex_start(0, m)
        for m in range(micro):
            combine(0, m, stat)

    @pl.when(last)
    def _():
        for m in range(micro):
            ubuf[m, rp - 16 : rp, :] = jnp.zeros((16, width), bf16)
            ubuf[m, 0:real, :] = cotangent[m]

    def forward(m):
        @pl.when(not_first)
        def _():
            loop(nw, lambda j: x_copy(m, j).wait_recv())
            st_copy(m).wait_recv()

        mean = stat[m, 0:1, :]
        inverse = stat[m, 1:2, :]
        aff[m] = (
            (xbuf[m].astype(f32) - mean) * inverse * gain[...] + shift[...]
        ).astype(bf16)

        def hidden_tile(j):
            before = jnp.dot(aff[m], w_in[0, :, cut(j, ht)], preferred_element_type=f32)
            bend = jnp.tanh(gelu_scale * (before + cubic_term * before * before * before))
            active[m, :, cut(j, ht)] = (0.5 * before * (1.0 + bend)).astype(bf16)
            slope[m, :, cut(j, ht)] = before

        loop(nh, hidden_tile)

        def out_tile(j):
            fresh = xbuf[m, :, cut(j, wt)].astype(f32) + jnp.dot(
                active[m], w_out[0, :, cut(j, wt)], preferred_element_type=f32
            )
            fresh = jnp.where(valid, fresh, 0.0).astype(bf16)
            out[0, m, :, cut(j, wt)] = fresh

            @pl.when(not_last)
            def _():
                x_copy(m, j).start()
                local_stats(1, m, j, fresh.astype(f32))

        loop(nw, out_tile)

        @pl.when(not_last)
        def _():
            ex_start(1, m)
            combine(1, m, stat_out)
            st_copy(m).start()

        def tail_tile(j):
            before = slope[m, :, cut(j, ht)]
            bend = jnp.tanh(gelu_scale * (before + cubic_term * before * before * before))
            slope[m, :, cut(j, ht)] = 0.5 * (1.0 + bend) + 0.5 * before * (
                1.0 - bend * bend
            ) * gelu_scale * (1.0 + 3.0 * cubic_term * before * before)
            act_t[m, cut(j, ht), :] = active[m, :, cut(j, ht)].T

        loop(nh, tail_tile)

        def turn_tile(j):
            aff_t[m, cut(j, wt), :] = aff[m, :, cut(j, wt)].T

        loop(nw, turn_tile)

    def backward(m):
        @pl.when(not_last)
        def _():
            loop(nw, lambda j: u_copy(m, j).wait_recv())

        def hidden_tile(j):
            pulled = across(ubuf[m], w_out[0, cut(j, ht), :])
            gb[m, :, cut(j, ht)] = (pulled * slope[m, :, cut(j, ht)]).astype(bf16)

        loop(nh, hidden_tile)

        def normed_of(j):
            return (
                xbuf[m, :, cut(j, wt)].astype(f32) - stat[m, 0:1, cut(j, wt)]
            ) * stat[m, 1:2, cut(j, wt)]

        def affine_tile(j):
            pulled = across(gb[m], w_in[0, cut(j, wt), :])
            ga_buf[:, cut(j, wt)] = pulled
            ex[2, m, me, 0:1, cut(j, wt)] = jnp.sum(pulled, axis=0, keepdims=True)
            ex[2, m, me, 1:2, cut(j, wt)] = jnp.sum(pulled * normed_of(j), axis=0, keepdims=True)

        loop(nw, affine_tile)
        ex_start(2, m)
        parts = ex_wait(2, m)
        ggain[...] += jnp.sum(parts[:, 1, :], axis=0, keepdims=True)
        gshift[...] += jnp.sum(parts[:, 0, :], axis=0, keepdims=True)

        def grad_tile(j):
            cols = cut(j, wt)
            sums = ex[2, m, :, :, cols]
            sum_grad = jnp.sum(sums[:, 0, :], axis=0, keepdims=True)
            sum_cross = jnp.sum(sums[:, 1, :], axis=0, keepdims=True)
            normed = normed_of(j)
            fresh = ubuf[m, :, cols].astype(f32) + stat[m, 1:2, cols] * gain[:, cols] * (
                ga_buf[:, cols] - sum_grad / rows - normed * (sum_cross / rows)
            )
            gin[0, m, :, cols] = jnp.where(valid, fresh, 0.0).astype(bf16)

            @pl.when(not_first)
            def _():
                u_copy(m, j).start()

        loop(nw, grad_tile)

    def step(t):
        ahead = jnp.where(last, lax.rem(t, 2) == 0, t < micro)
        m = jnp.where(last, t // 2, lax.rem(t, micro))

        @pl.when(ahead)
        def _():
            forward(m)

        @pl.when(jnp.logical_not(ahead))
        def _():
            backward(m)

    loop(2 * micro, step)

    core = lax.rem(me, 2)
    chip = me // 2
    my_y = chip // nx
    my_x = lax.rem(chip, nx)

    def place(y, x, c):
        return (y * nx + x) * 2 + c

    plans = (
        (0, ny, nx, my_y, my_x, lambda a, b, c: place(a, b, c), act_t, ubuf,
         send_o, keep_o, r0_o, r1_o, r2_o, red_out, hidden // n),
        (1, nx, ny, my_x, my_y, lambda a, b, c: place(b, a, c), aff_t, gb,
         send_i, keep_i, r0_i, r1_i, r2_i, red_in, width // n),
    )

    def copy0(g, plan, s):
        return pltpu.make_async_remote_copy(
            src_ref=plan[8].at[s], dst_ref=plan[10].at[s],
            send_sem=s0.at[g, s], recv_sem=q0.at[g, s],
            device_id={"dp": chip * 2 + 1 - core}, device_id_type=MESH,
        )

    def copy1(g, plan, k, slot):
        na, nb, a, b, where = plan[1:6]
        to = lax.rem(a + k + 1, na)
        return pltpu.make_async_remote_copy(
            src_ref=plan[8].at[pl.ds(to * nb, nb)], dst_ref=plan[11].at[k],
            send_sem=s1.at[g, k], recv_sem=q1.at[g, k],
            device_id={"dp": where(to, b, core)}, device_id_type=MESH,
        )

    def copy2(g, plan, k):
        na, nb, a, b, where = plan[1:6]
        to = lax.rem(b + k + 1, nb)
        return pltpu.make_async_remote_copy(
            src_ref=plan[8].at[a * nb + to], dst_ref=plan[12].at[k],
            send_sem=s2.at[g, k], recv_sem=q2.at[g, k],
            device_id={"dp": where(a, to, core)}, device_id_type=MESH,
        )

    for plan in plans:
        g, na, nb, a, b, where, left, right, send, keep, r0, r1, r2, red, block = plan

        def partial(owner):
            total = jnp.dot(left[0, cut(owner, block), :], right[0], preferred_element_type=f32)
            for m in range(1, micro):
                total += jnp.dot(left[m, cut(owner, block), :], right[m], preferred_element_type=f32)
            return total

        def away(s):
            send[s] = partial(where(s // nb, lax.rem(s, nb), 1 - core)).astype(bf16)
            copy0(g, plan, s).start()

        loop(na * nb, away)

    for plan in plans:
        g, na, nb, a, b, where, left, right, send, keep, r0, r1, r2, red, block = plan

        def partial(owner):
            total = jnp.dot(left[0, cut(owner, block), :], right[0], preferred_element_type=f32)
            for m in range(1, micro):
                total += jnp.dot(left[m, cut(owner, block), :], right[m], preferred_element_type=f32)
            return total

        def other(k):
            to = lax.rem(a + k + 1, na)

            def one(i):
                s = to * nb + i
                copy0(g, plan, s).wait()
                total = partial(where(to, i, core)) + r0[s].astype(f32)
                send[s] = total.astype(bf16)

            loop(nb, one)
            copy1(g, plan, k, 0).start()

        loop(na - 1, other)

        def own(i):
            s = a * nb + i
            copy0(g, plan, s).wait()
            keep[i] = partial(where(a, i, core)) + r0[s].astype(f32)

        loop(nb, own)

    for plan in plans:
        g, na, nb, a, b, where, left, right, send, keep, r0, r1, r2, red, block = plan
        loop(na - 1, lambda k: copy1(g, plan, k, 0).wait())

        def across_sum(to):
            total = keep[to]
            for k in range(na - 1):
                total += r1[k, to].astype(f32)
            return total

        def other2(k):
            to = lax.rem(b + k + 1, nb)
            send[a * nb + to] = across_sum(to).astype(bf16)
            copy2(g, plan, k).start()

        loop(nb - 1, other2)
        keep[b] = across_sum(b)

    for plan in plans:
        g, na, nb, a, b, where, left, right, send, keep, r0, r1, r2, red, block = plan
        loop(nb - 1, lambda k: copy2(g, plan, k).wait())
        total = keep[b]
        for k in range(nb - 1):
            total += r2[k].astype(f32)
        red[0] = total

    @pl.when(not_last)
    def _():
        for m in range(micro):
            loop(nw, lambda j: x_copy(m, j).wait_send())
            st_copy(m).wait_send()

    @pl.when(not_first)
    def _():
        for m in range(micro):
            loop(nw, lambda j: u_copy(m, j).wait_send())


def local(images, cotangent, w_in, w_out, gain, shift):
    sections = lax.axis_size("section")
    n = lax.axis_size("dp")
    micro, real, width = images.shape
    hidden = w_in.shape[2]
    rp = -(-real // 16) * 16
    chips = n // 2
    ny = near_square(chips)
    nx = chips // ny
    nw = width // min(256, width)
    bi, bo = width // n, hidden // n
    top = max(nx, ny)
    sizes = (sections, n, micro, real, rp, width, hidden, nx, ny)
    shape = jax.ShapeDtypeStruct
    vmem = pl.BlockSpec(memory_space=pltpu.VMEM)
    dma = pltpu.SemaphoreType.DMA
    scratch = [
        pltpu.VMEM((micro, rp, width), bf16),
        pltpu.VMEM((micro, rp, width), bf16),
        pltpu.VMEM((micro, 2, width), f32),
        pltpu.VMEM((micro, 2, width), f32),
        pltpu.VMEM((3, micro, n, 2, width), f32),
        pltpu.VMEM((micro, rp, width), bf16),
        pltpu.VMEM((micro, rp, hidden), bf16),
        pltpu.VMEM((micro, rp, hidden), f32),
        pltpu.VMEM((micro, rp, hidden), bf16),
        pltpu.VMEM((rp, width), f32),
        pltpu.VMEM((micro, hidden, rp), bf16),
        pltpu.VMEM((micro, width, rp), bf16),
    ]
    for na, nb, block, cols in ((nx, ny, bi, hidden), (ny, nx, bo, width)):
        scratch += [
            pltpu.VMEM((chips, block, cols), bf16),
            pltpu.VMEM((nb, block, cols), f32),
            pltpu.VMEM((chips, block, cols), bf16),
            pltpu.VMEM((max(na - 1, 1), nb, block, cols), bf16),
            pltpu.VMEM((max(nb - 1, 1), block, cols), bf16),
        ]
    scratch += [
        dma((micro, nw)), dma((micro, nw)), dma((micro, nw)), dma((micro, nw)),
        dma((micro,)), dma((micro,)),
        dma((3, micro, n - 1)), dma((3, micro, n - 1)),
        dma((2, chips)), dma((2, chips)),
        dma((2, top)), dma((2, top)), dma((2, top)), dma((2, top)),
    ]
    flops = 12 * micro * real * width * hidden
    outs = pl.pallas_call(
        functools.partial(kernel, sizes),
        out_shape=(
            shape((1, micro, rp, width), bf16),
            shape((1, micro, rp, width), bf16),
            shape((1, bi, hidden), f32),
            shape((1, bo, width), f32),
            shape((1, width), f32),
            shape((1, width), f32),
        ),
        in_specs=[vmem] * 6,
        out_specs=(vmem,) * 6,
        scratch_shapes=scratch,
        compiler_params=pltpu.CompilerParams(
            collective_id=0, has_side_effects=True, vmem_limit_bytes=60 * 1024 * 1024
        ),
        cost_estimate=pl.CostEstimate(
            flops=flops, bytes_accessed=8 * width * hidden, transcendentals=2 * micro * real * hidden
        ),
        name="relay",
    )(images, cotangent, w_in, w_out, gain, shift)
    return (outs[0][:, :, :real], outs[1][:, :, :real], *outs[2:])


def solution(mesh):
    placed = (
        P(None, "dp", None),
        P(None, "dp", None),
        P("section", None, None),
        P("section", None, None),
        P("section", None),
        P("section", None),
    )
    return jax.shard_map(
        local,
        mesh=mesh,
        in_specs=placed,
        out_specs=(
            P("section", None, "dp", None),
            P("section", None, "dp", None),
            P("section", "dp", None),
            P("section", "dp", None),
            P("section", None),
            P("section", None),
        ),
        check_vma=False,
    )
```

time: 503 us -> 197 us (0.39); the launches traced: 493 us -> 197 us
  Pallas kernels: 0 us -> 183 us
  waiting for transfers between devices: 130 us -> 0 us
  blocking collectives: 125 us -> 0 us
  matrix products: 104 us -> 0 us
  local copies, waits for them, and re-layouts: 57.2 us -> 13.6 us
  other arithmetic: 37.6 us -> 0 us
  starting transfers between devices: 23.2 us -> 0 us
  between operations: 15.8 us -> 0.68 us
    pallas_call x0 -> x1, Pallas kernels: none -> 183 us  [local(): pl.pallas_call(functools.partial(kernel, sizes), out_shape=(shape((1, mic...]
    psum x10 -> x0, blocking collectives: 125 us -> none  [the longest x5 63.8 us: statistics(): lax.psum((jnp.sum(inputs, axis=0), jnp.sum(inputs * inputs, axis=0)), 'dp')]
    dot_general x30 -> x0, matrix products: 104 us -> none  [the longest x5 25.7 us: local(): jnp.dot(affine.T, grad_before, preferred_element_type=jnp.float32)]
    reduce_scatter x2 -> x0, waiting for transfers between devices: 86 us -> none  [the longest x1 75.8 us: local(): lax.psum_scatter(grad_out, 'dp', scatter_dimension=0, tiled=True)]
    ppermute x8 -> x0, waiting for transfers between devices: 44.3 us -> none  [from_behind(): return lax.ppermute(block, axis, route)]
    dynamic_update_slice x20 -> x0, other arithmetic: 31.5 us -> none  [place(): lax.dynamic_update_index_in_dim(buffer, jnp.where(valid, fresh, kept), sl...]
    dynamic_slice x26 -> x0, local copies, waits for them, and re-layouts: 25.1 us -> none  [pick(): return lax.dynamic_index_in_dim(buffer, slot, 0, keepdims=False)]
    ppermute x8 -> x0, starting transfers between devices: 22.9 us -> none  [from_behind(): return lax.ppermute(block, axis, route)]
  transfers between devices with their start and end apart: 10 -> 0, of which waited for: 9 -> 0; matrix products, arithmetic and copies ran while one was open for 17% -> 0% of each run, Pallas kernels for 0% -> 0%
where the time goes in v1:
time: 197 us
  Pallas kernels  183 us (93%)
  local copies, waits for them, and re-layouts  13.6 us (7%)
    pallas_call x1, Pallas kernels, local(): pl.pallas_call(functools.partial(kernel, sizes), out_shape=(shape((1, mic...  183 us
    unnamed x16, local copies, waits for them, and re-layouts  11.1 us

profile of v1, /device:TPU:0, one launch (start us, length us, event | category | flops | bytes accessed | tf_op | source)
XLA Modules:
  0.0 196.8 jit_solution(17420094167267359200)
XLA Ops:
  0.6 2.2 %copy.12.images = bf16[2,197,1024]{2,1,0:T(8,128)(2,1)} copy(bf16[2,197,1024]{2,0,1:T(2,128)(2,1)} %param.6) | data formatting | bytes 1613824 | tf_op args[0]
  2.9 2.2 %copy.13.cotangent = bf16[2,197,1024]{2,1,0:T(8,128)(2,1)} copy(bf16[2,197,1024]{2,0,1:T(2,128)(2,1)} %param.7) | data formatting | bytes 1613824 | tf_op args[1]
  5.1 182.5 %relay.1 = (bf16[1,2,208,1024]{3,2,1,0:T(8,128)(2,1)}, bf16[1,2,208,1024]{3,2,1,0:T(8,128)(2,1)}, f32[1,128,2048]{2,1,0:T(8,128)}, f32[1,256,1024]{2,1,0:T(8,128...) custom-call(bf16[2,197,1024]{2,1,0:T(8,128)(2,1)} %copy.12.images, bf16[2,197,1024]{2,1,0:T(8,128)(2,1)} %copy.13.cotangent, ...), custom_call_target="tpu_custom_call" | custom-call | flops 9915334656 | bytes 16777216 | tf_op jit(solution)/shard_map/relay/pallas_call | solution.py:458
  187.6 0.0 copy-start.1
  187.7 0.0 copy-start
  187.7 1.3 slice.6
  189.0 0.0 copy-start.3
  189.0 0.0 copy-start.2
  189.0 1.7 copy.14
  190.8 1.2 slice.7
  192.0 1.7 copy.15
  193.7 0.0 copy-done.1
  193.7 1.0 copy.20
  194.7 0.0 copy-done
  194.7 1.0 copy.21
  195.6 0.0 copy-done.3
  195.6 0.6 copy.22
  196.2 0.0 copy-done.2
  196.2 0.6 copy.23
Async XLA Ops:
  187.6 6.0 %copy-start.1 = (f32[1,128,2048]{2,1,0:T(8,128)S(1)}, f32[1,128,2048]{2,1,0:T(8,128)}, u32[]{:S(2)}) copy-start(f32[1,128,2048]{2,1,0:T(8,128)} %get-tuple-element.32) | copy-start | bytes 3145732
  187.7 7.0 %copy-start = (f32[1,256,1024]{2,1,0:T(8,128)S(1)}, f32[1,256,1024]{2,1,0:T(8,128)}, u32[]{:S(2)}) copy-start(f32[1,256,1024]{2,1,0:T(8,128)} %get-tuple-element.33) | copy-start | bytes 3145732
  189.0 6.6 %copy-start.3 = (f32[1,1024]{1,0:T(1,128)S(1)}, f32[1,1024]{1,0:T(1,128)}, u32[]{:S(2)}) copy-start(f32[1,1024]{1,0:T(1,128)} %get-tuple-element.34) | copy-start | bytes 12292
  189.0 7.2 %copy-start.2 = (f32[1,1024]{1,0:T(1,128)S(1)}, f32[1,1024]{1,0:T(1,128)}, u32[]{:S(2)}) copy-start(f32[1,1024]{1,0:T(1,128)} %get-tuple-element.35) | copy-start | bytes 12292

commit v2 on v1

--- a/solution.py
+++ b/solution.py
@@ -30,7 +30,14 @@
     lax.fori_loop(0, count, step, 0)
 
 
+def unrolled(count, body):
+    for i in range(count):
+        body(i)
+
+
 def cut(j, size):
+    if isinstance(j, int):
+        return pl.ds(j * size, size)
     return pl.ds(pl.multiple_of(j * size, size), size)
 
 
@@ -42,7 +49,7 @@
     sizes,
     images, cotangent, w_in, w_out, gain, shift,
     out, gin, red_in, red_out, ggain, gshift,
-    xbuf, ubuf, stat, stat_out, ex, aff, active, slope, gb, ga_buf, act_t, aff_t,
+    xbuf, ubuf, xout, uout, stat, stat_out, ex, aff, active, slope, gb, ga_buf, act_t, aff_t,
     send_i, keep_i, r0_i, r1_i, r2_i,
     send_o, keep_o, r0_o, r1_o, r2_o,
     x_send, x_recv, u_send, u_recv, st_send, st_recv, ex_send, ex_recv,
@@ -121,7 +128,7 @@
 
     def x_copy(m, j):
         return pltpu.make_async_remote_copy(
-            src_ref=out.at[0, m, :, cut(j, wt)],
+            src_ref=xout.at[m, :, cut(j, wt)],
             dst_ref=xbuf.at[m, :, cut(j, wt)],
             send_sem=x_send.at[m, j],
             recv_sem=x_recv.at[m, j],
@@ -131,7 +138,7 @@
 
     def u_copy(m, j):
         return pltpu.make_async_remote_copy(
-            src_ref=gin.at[0, m, :, cut(j, wt)],
+            src_ref=uout.at[m, :, cut(j, wt)],
             dst_ref=ubuf.at[m, :, cut(j, wt)],
             send_sem=u_send.at[m, j],
             recv_sem=u_recv.at[m, j],
@@ -190,14 +197,15 @@
             active[m, :, cut(j, ht)] = (0.5 * before * (1.0 + bend)).astype(bf16)
             slope[m, :, cut(j, ht)] = before
 
-        loop(nh, hidden_tile)
+        unrolled(nh, hidden_tile)
 
         def out_tile(j):
             fresh = xbuf[m, :, cut(j, wt)].astype(f32) + jnp.dot(
                 active[m], w_out[0, :, cut(j, wt)], preferred_element_type=f32
             )
             fresh = jnp.where(valid, fresh, 0.0).astype(bf16)
-            out[0, m, :, cut(j, wt)] = fresh
+            xout[m, :, cut(j, wt)] = fresh
+            out[0, m, :, cut(j, wt)] = fresh[0:real]
 
             @pl.when(not_last)
             def _():
@@ -227,50 +235,64 @@
 
         loop(nw, turn_tile)
 
-    def backward(m):
+    def receive(m):
         @pl.when(not_last)
         def _():
             loop(nw, lambda j: u_copy(m, j).wait_recv())
 
+    def hidden_grad(m):
         def hidden_tile(j):
             pulled = across(ubuf[m], w_out[0, cut(j, ht), :])
             gb[m, :, cut(j, ht)] = (pulled * slope[m, :, cut(j, ht)]).astype(bf16)
 
-        loop(nh, hidden_tile)
-
+        unrolled(nh, hidden_tile)
+
+    def input_grad(m):
         def normed_of(j):
             return (
                 xbuf[m, :, cut(j, wt)].astype(f32) - stat[m, 0:1, cut(j, wt)]
             ) * stat[m, 1:2, cut(j, wt)]
 
         def affine_tile(j):
-            pulled = across(gb[m], w_in[0, cut(j, wt), :])
-            ga_buf[:, cut(j, wt)] = pulled
-            ex[2, m, me, 0:1, cut(j, wt)] = jnp.sum(pulled, axis=0, keepdims=True)
-            ex[2, m, me, 1:2, cut(j, wt)] = jnp.sum(pulled * normed_of(j), axis=0, keepdims=True)
-
-        loop(nw, affine_tile)
+            cols = cut(j, wt)
+            pulled = across(gb[m], w_in[0, cols, :])
+            ga_buf[:, cols] = pulled
+
+            ex[2, m, me, 0:1, cols] = jnp.sum(pulled, axis=0, keepdims=True)
+            ex[2, m, me, 1:2, cols] = jnp.sum(pulled * normed_of(j), axis=0, keepdims=True)
+
+        unrolled(nw, affine_tile)
         ex_start(2, m)
         parts = ex_wait(2, m)
-        ggain[...] += jnp.sum(parts[:, 1, :], axis=0, keepdims=True)
-        gshift[...] += jnp.sum(parts[:, 0, :], axis=0, keepdims=True)
+        sum_cross = jnp.sum(parts[:, 1, :], axis=0, keepdims=True)
+        sum_grad = jnp.sum(parts[:, 0, :], axis=0, keepdims=True)
+
+        ggain[...] += sum_cross
+        gshift[...] += sum_grad
 
         def grad_tile(j):
             cols = cut(j, wt)
             sums = ex[2, m, :, :, cols]
-            sum_grad = jnp.sum(sums[:, 0, :], axis=0, keepdims=True)
-            sum_cross = jnp.sum(sums[:, 1, :], axis=0, keepdims=True)
-            normed = normed_of(j)
+            part_grad = jnp.sum(sums[:, 0, :], axis=0, keepdims=True)
+            part_cross = jnp.sum(sums[:, 1, :], axis=0, keepdims=True)
             fresh = ubuf[m, :, cols].astype(f32) + stat[m, 1:2, cols] * gain[:, cols] * (
-                ga_buf[:, cols] - sum_grad / rows - normed * (sum_cross / rows)
+                ga_buf[:, cols] - part_grad / rows - normed_of(j) * (part_cross / rows)
             )
-            gin[0, m, :, cols] = jnp.where(valid, fresh, 0.0).astype(bf16)
+            fresh = jnp.where(valid, fresh, 0.0).astype(bf16)
+            uout[m, :, cols] = fresh
 
             @pl.when(not_first)
             def _():
                 u_copy(m, j).start()
 
+            gin[0, m, :, cols] = fresh[0:real]
+
         loop(nw, grad_tile)
+
+    def backward(m):
+        receive(m)
+        hidden_grad(m)
+        input_grad(m)
 
     def step(t):
         ahead = jnp.where(last, lax.rem(t, 2) == 0, t < micro)
@@ -284,7 +306,7 @@
         def _():
             backward(m)
 
-    loop(2 * micro, step)
+    loop(2 * micro - 1, step)
 
     core = lax.rem(me, 2)
     chip = me // 2
@@ -326,50 +348,78 @@
             device_id={"dp": where(a, to, core)}, device_id_type=MESH,
         )
 
-    for plan in plans:
+    def partial(plan, owner):
+        left, right, block = plan[6], plan[7], plan[14]
+        total = jnp.dot(left[0, cut(owner, block), :], right[0], preferred_element_type=f32)
+        for m in range(1, micro):
+            total += jnp.dot(left[m, cut(owner, block), :], right[m], preferred_element_type=f32)
+        return total
+
+    def send_away(plan):
+        g, na, nb, a, b, where = plan[:6]
+        send = plan[8]
+
+        def away(s):
+            owner = where(s // nb, lax.rem(s, nb), 1 - core)
+            send[s] = partial(plan, owner).astype(bf16)
+            copy0(g, plan, s).start()
+
+        loop(na * nb, away)
+
+    def send_first(plan):
         g, na, nb, a, b, where, left, right, send, keep, r0, r1, r2, red, block = plan
-
-        def partial(owner):
-            total = jnp.dot(left[0, cut(owner, block), :], right[0], preferred_element_type=f32)
-            for m in range(1, micro):
-                total += jnp.dot(left[m, cut(owner, block), :], right[m], preferred_element_type=f32)
-            return total
-
-        def away(s):
-            send[s] = partial(where(s // nb, lax.rem(s, nb), 1 - core)).astype(bf16)
-            copy0(g, plan, s).start()
-
-        loop(na * nb, away)
-
-    for plan in plans:
-        g, na, nb, a, b, where, left, right, send, keep, r0, r1, r2, red, block = plan
-
-        def partial(owner):
-            total = jnp.dot(left[0, cut(owner, block), :], right[0], preferred_element_type=f32)
-            for m in range(1, micro):
-                total += jnp.dot(left[m, cut(owner, block), :], right[m], preferred_element_type=f32)
-            return total
 
         def other(k):
             to = lax.rem(a + k + 1, na)
 
             def one(i):
                 s = to * nb + i
+                total = partial(plan, where(to, i, core))
                 copy0(g, plan, s).wait()
-                total = partial(where(to, i, core)) + r0[s].astype(f32)
-                send[s] = total.astype(bf16)
+                send[s] = (total + r0[s].astype(f32)).astype(bf16)
 
             loop(nb, one)
             copy1(g, plan, k, 0).start()
 
         loop(na - 1, other)
 
+    def own_first(plan):
+        g, na, nb, a, b, where, left, right, send, keep, r0, r1, r2, red, block = plan
+
         def own(i):
             s = a * nb + i
+            total = partial(plan, where(a, i, core))
             copy0(g, plan, s).wait()
-            keep[i] = partial(where(a, i, core)) + r0[s].astype(f32)
+            keep[i] = total + r0[s].astype(f32)
 
         loop(nb, own)
+
+    final = micro - 1
+    receive(final)
+
+    @pl.when(first)
+    def _():
+        send_away(plans[0])
+
+    hidden_grad(final)
+
+    @pl.when(first)
+    def _():
+        send_away(plans[1])
+        send_first(plans[0])
+        send_first(plans[1])
+
+    input_grad(final)
+
+    @pl.when(not_first)
+    def _():
+        send_away(plans[0])
+        send_away(plans[1])
+        send_first(plans[0])
+        send_first(plans[1])
+
+    own_first(plans[0])
+    own_first(plans[1])
 
     for plan in plans:
         g, na, nb, a, b, where, left, right, send, keep, r0, r1, r2, red, block = plan
@@ -426,6 +476,8 @@
     vmem = pl.BlockSpec(memory_space=pltpu.VMEM)
     dma = pltpu.SemaphoreType.DMA
     scratch = [
+        pltpu.VMEM((micro, rp, width), bf16),
+        pltpu.VMEM((micro, rp, width), bf16),
         pltpu.VMEM((micro, rp, width), bf16),
         pltpu.VMEM((micro, rp, width), bf16),
         pltpu.VMEM((micro, 2, width), f32),
@@ -458,8 +510,8 @@
     outs = pl.pallas_call(
         functools.partial(kernel, sizes),
         out_shape=(
-            shape((1, micro, rp, width), bf16),
-            shape((1, micro, rp, width), bf16),
+            shape((1, micro, real, width), bf16),
+            shape((1, micro, real, width), bf16),
             shape((1, bi, hidden), f32),
             shape((1, bo, width), f32),
             shape((1, width), f32),
@@ -476,7 +528,7 @@
         ),
         name="relay",
     )(images, cotangent, w_in, w_out, gain, shift)
-    return (outs[0][:, :, :real], outs[1][:, :, :real], *outs[2:])
+    return tuple(outs)
 
 
 def solution(mesh):

time: 197 us -> 188 us (0.954)
  Pallas kernels: 183 us -> 172 us
    pallas_call x1, Pallas kernels: 183 us -> 172 us  [local(): pl.pallas_call(functools.partial(kernel, sizes), out_shape=(shape((1, mic...]
    pallas_call x0 -> x2, local copies, waits for them, and re-layouts: none -> 5.81 us  [local(): pl.pallas_call(functools.partial(kernel, sizes), out_shape=(shape((1, mic...]
    slice x2 -> x0, local copies, waits for them, and re-layouts: 2.55 us -> none  [local(): return (outs[0][:, :, :real], outs[1][:, :, :real], *outs[2:])]
    unnamed x16 -> x12, local copies, waits for them, and re-layouts: 11.1 us -> 8.95 us
where the time goes in v2:
time: 188 us
  Pallas kernels  172 us (91%)
  local copies, waits for them, and re-layouts  14.8 us (8%)
    pallas_call x1, Pallas kernels, local(): pl.pallas_call(functools.partial(kernel, sizes), out_shape=(shape((1, mic...  172 us
    unnamed x12, local copies, waits for them, and re-layouts  8.95 us
    pallas_call x2, local copies, waits for them, and re-layouts, local(): pl.pallas_call(functools.partial(kernel, sizes), out_shape=(shape((1, mic...  5.81 us

profile of v2, /device:TPU:0, one launch (start us, length us, event | category | flops | bytes accessed | tf_op | source)
XLA Modules:
  0.0 187.5 jit_solution(2842314210317250654)
XLA Ops:
  0.6 2.2 %copy.12.images = bf16[2,197,1024]{2,1,0:T(8,128)(2,1)} copy(bf16[2,197,1024]{2,0,1:T(2,128)(2,1)} %param.6) | data formatting | bytes 1613824 | tf_op args[0]
  2.9 2.2 %copy.13.cotangent = bf16[2,197,1024]{2,1,0:T(8,128)(2,1)} copy(bf16[2,197,1024]{2,0,1:T(2,128)(2,1)} %param.7) | data formatting | bytes 1613824 | tf_op args[1]
  5.1 172.1 %relay.1 = (bf16[1,2,197,1024]{3,2,1,0:T(8,128)(2,1)}, bf16[1,2,197,1024]{3,2,1,0:T(8,128)(2,1)}, f32[1,128,2048]{2,1,0:T(8,128)}, f32[1,256,1024]{2,1,0:T(8,128...) custom-call(bf16[2,197,1024]{2,1,0:T(8,128)(2,1)} %copy.12.images, bf16[2,197,1024]{2,1,0:T(8,128)(2,1)} %copy.13.cotangent, ...), custom_call_target="tpu_custom_call" | custom-call | flops 9915334656 | bytes 16777216 | tf_op jit(solution)/shard_map/relay/pallas_call | solution.py:510
  177.2 0.0 copy-start
  177.2 0.0 copy-start.2
  177.2 0.0 copy-start.1
  177.3 2.9 %copy.14 = bf16[1,2,197,1024]{3,1,2,0:T(2,128)(2,1)} copy(bf16[1,2,197,1024]{3,2,1,0:T(8,128)(2,1)} %get-tuple-element.6) | data formatting | bytes 1613824 | tf_op jit(solution)/shard_map/relay/pallas_call | solution.py:510
  180.2 2.9 %copy.15 = bf16[1,2,197,1024]{3,1,2,0:T(2,128)(2,1)} copy(bf16[1,2,197,1024]{3,2,1,0:T(8,128)(2,1)} %get-tuple-element.7) | data formatting | bytes 1613824 | tf_op jit(solution)/shard_map/relay/pallas_call | solution.py:510
  183.1 2.3 %copy.20 = f32[1,128,2048]{2,1,0:T(8,128)} copy(f32[1,128,2048]{2,1,0:T(8,128)} %get-tuple-element.20) | data formatting | bytes 2097152
  185.4 0.0 copy-done
  185.4 1.0 copy.21
  186.3 0.0 copy-done.2
  186.3 0.6 copy.22
  186.9 0.0 copy-done.1
  186.9 0.6 copy.23
Async XLA Ops:
  177.2 8.1 %copy-start = (f32[1,256,1024]{2,1,0:T(8,128)S(1)}, f32[1,256,1024]{2,1,0:T(8,128)}, u32[]{:S(2)}) copy-start(f32[1,256,1024]{2,1,0:T(8,128)} %get-tuple-element.21) | copy-start | bytes 3145732
  177.2 9.1 %copy-start.2 = (f32[1,1024]{1,0:T(1,128)S(1)}, f32[1,1024]{1,0:T(1,128)}, u32[]{:S(2)}) copy-start(f32[1,1024]{1,0:T(1,128)} %get-tuple-element.22) | copy-start | bytes 12292
  177.2 9.7 %copy-start.1 = (f32[1,1024]{1,0:T(1,128)S(1)}, f32[1,1024]{1,0:T(1,128)}, u32[]{:S(2)}) copy-start(f32[1,1024]{1,0:T(1,128)} %get-tuple-element.23) | copy-start | bytes 12292

commit v3 on v2

--- a/solution.py
+++ b/solution.py
@@ -163,7 +163,7 @@
     def _():
         for m in range(micro):
             xbuf[m, rp - 16 : rp, :] = jnp.zeros((16, width), bf16)
-            xbuf[m, 0:real, :] = images[m]
+            xbuf[m, 0:real, :] = images[:, m, :]
 
             def tile(j):
                 local_stats(0, m, j, xbuf[m, :, cut(j, wt)].astype(f32))
@@ -177,7 +177,7 @@
     def _():
         for m in range(micro):
             ubuf[m, rp - 16 : rp, :] = jnp.zeros((16, width), bf16)
-            ubuf[m, 0:real, :] = cotangent[m]
+            ubuf[m, 0:real, :] = cotangent[:, m, :]
 
     def forward(m):
         @pl.when(not_first)
@@ -226,14 +226,23 @@
             slope[m, :, cut(j, ht)] = 0.5 * (1.0 + bend) + 0.5 * before * (
                 1.0 - bend * bend
             ) * gelu_scale * (1.0 + 3.0 * cubic_term * before * before)
+
+        loop(nh, tail_tile)
+
+        @pl.when(not_last)
+        def _():
+            turn(m)
+
+    def turn(m):
+        def active_tile(j):
             act_t[m, cut(j, ht), :] = active[m, :, cut(j, ht)].T
 
-        loop(nh, tail_tile)
-
-        def turn_tile(j):
+        loop(nh, active_tile)
+
+        def affine_tile(j):
             aff_t[m, cut(j, wt), :] = aff[m, :, cut(j, wt)].T
 
-        loop(nw, turn_tile)
+        loop(nw, affine_tile)
 
     def receive(m):
         @pl.when(not_last)
@@ -294,6 +303,10 @@
         hidden_grad(m)
         input_grad(m)
 
+        @pl.when(last)
+        def _():
+            turn(m)
+
     def step(t):
         ahead = jnp.where(last, lax.rem(t, 2) == 0, t < micro)
         m = jnp.where(last, t // 2, lax.rem(t, micro))
@@ -410,6 +423,10 @@
         send_first(plans[1])
 
     input_grad(final)
+
+    @pl.when(last)
+    def _():
+        turn(final)
 
     @pl.when(not_first)
     def _():
@@ -527,7 +544,7 @@
             flops=flops, bytes_accessed=8 * width * hidden, transcendentals=2 * micro * real * hidden
         ),
         name="relay",
-    )(images, cotangent, w_in, w_out, gain, shift)
+    )(jnp.swapaxes(images, 0, 1), jnp.swapaxes(cotangent, 0, 1), w_in, w_out, gain, shift)
     return tuple(outs)
 
 

time: 188 us -> 183 us (0.973)
  local copies, waits for them, and re-layouts: 14.8 us -> 10.3 us
    unnamed x12 -> x10, local copies, waits for them, and re-layouts: 8.95 us -> 4.46 us
where the time goes in v3:
time: 183 us
  Pallas kernels  172 us (94%)
  local copies, waits for them, and re-layouts  10.3 us (6%)
    pallas_call x1, Pallas kernels, local(): pl.pallas_call(functools.partial(kernel, sizes), out_shape=(shape((1, mic...  172 us
    pallas_call x2, local copies, waits for them, and re-layouts, local(): pl.pallas_call(functools.partial(kernel, sizes), out_shape=(shape((1, mic...  5.81 us
    unnamed x10, local copies, waits for them, and re-layouts  4.46 us

profile of v3, /device:TPU:0, one launch (start us, length us, event | category | flops | bytes accessed | tf_op | source)
XLA Modules:
  0.0 182.9 jit_solution(11817263113295879177)
XLA Ops:
  0.6 171.9 %relay.1 = (bf16[1,2,197,1024]{3,2,1,0:T(8,128)(2,1)}, bf16[1,2,197,1024]{3,2,1,0:T(8,128)(2,1)}, f32[1,128,2048]{2,1,0:T(8,128)}, f32[1,256,1024]{2,1,0:T(8,128...) custom-call(bf16[197,2,1024]{2,1,0:T(2,128)(2,1)} %bitcast.2, bf16[197,2,1024]{2,1,0:T(2,128)(2,1)} %bitcast.3, ...), custom_call_target="tpu_custom_call" | custom-call | flops 9915334656 | bytes 16777216 | tf_op jit(solution)/shard_map/relay/pallas_call | solution.py:527
  172.6 0.0 copy-start
  172.6 0.0 copy-start.2
  172.6 0.0 copy-start.1
  172.6 2.9 %copy.12 = bf16[1,2,197,1024]{3,1,2,0:T(2,128)(2,1)} copy(bf16[1,2,197,1024]{3,2,1,0:T(8,128)(2,1)} %get-tuple-element.6) | data formatting | bytes 1613824 | tf_op jit(solution)/shard_map/relay/pallas_call | solution.py:527
  175.6 2.9 %copy.13 = bf16[1,2,197,1024]{3,1,2,0:T(2,128)(2,1)} copy(bf16[1,2,197,1024]{3,2,1,0:T(8,128)(2,1)} %get-tuple-element.7) | data formatting | bytes 1613824 | tf_op jit(solution)/shard_map/relay/pallas_call | solution.py:527
  178.4 2.3 %copy.18 = f32[1,128,2048]{2,1,0:T(8,128)} copy(f32[1,128,2048]{2,1,0:T(8,128)} %get-tuple-element.20) | data formatting | bytes 2097152
  180.7 0.0 copy-done
  180.7 1.0 copy.19
  181.7 0.0 copy-done.2
  181.7 0.6 copy.20
  182.3 0.0 copy-done.1
  182.3 0.6 copy.21
Async XLA Ops:
  172.6 8.1 %copy-start = (f32[1,256,1024]{2,1,0:T(8,128)S(1)}, f32[1,256,1024]{2,1,0:T(8,128)}, u32[]{:S(2)}) copy-start(f32[1,256,1024]{2,1,0:T(8,128)} %get-tuple-element.21) | copy-start | bytes 3145732
  172.6 9.1 %copy-start.2 = (f32[1,1024]{1,0:T(1,128)S(1)}, f32[1,1024]{1,0:T(1,128)}, u32[]{:S(2)}) copy-start(f32[1,1024]{1,0:T(1,128)} %get-tuple-element.22) | copy-start | bytes 12292
  172.6 9.7 %copy-start.1 = (f32[1,1024]{1,0:T(1,128)S(1)}, f32[1,1024]{1,0:T(1,128)}, u32[]{:S(2)}) copy-start(f32[1,1024]{1,0:T(1,128)} %get-tuple-element.23) | copy-start | bytes 12292
